TPU v7x, 512 devices: a whole 4x4x16 slice. The times are simulated.
512 devices in a mesh: seq: 8 (over y, core), head: 64 (over z, x).
Axes of the slice: x: 4, y: 4, z: 16, core: 2. Of those that a mesh axis runs over, the one named last changes fastest.
Arguments:
- tokens: bfloat16 [8192, 2048], P('seq', 'head'), may hold values from -6 to 6
- z_weight: bfloat16 [2048, 4096], P(None, 'head'), may hold values from -0.125 to 0.125
- x_weight: bfloat16 [2048, 4096], P(None, 'head'), may hold values from -0.79549513 to 0.79549513
- bc_weight: bfloat16 [2048, 256], replicated, may hold values from -0.125 to 0.125
- step_weight: bfloat16 [2048, 64], P(None, 'head'), may hold values from -0.125 to 0.125
- x_kernel: float32 [4, 4096], P(None, 'head'), may hold values from -3 to 3
- bc_kernel: float32 [4, 256], replicated, may hold values from -3 to 3
- step_bias: float32 [64], P('head'), may hold values from -9 to -3
- log_decay: float32 [64], P('head'), may hold values from 0 to 1.5
- skip_gain: float32 [64], P('head'), may hold values from 0.2 to 0.8
- norm_gain: bfloat16 [4096], P('head'), may hold values from 0.099609375 to 1.8984375
- out_weight: bfloat16 [4096, 2048], P('head'), may hold values from -0.09375 to 0.09375
Outputs:
- mixed: bfloat16 [8192, 2048], P('seq', 'head')
All inputs are finite; a program needn't handle non-finite values.
Results may differ from a plain program's by a relative error of at most 0.017.
Values may be sent and summed in bfloat16 or wider, within the bound.
A program may use at most 64 MiB of HBM per device.

v0:
```python
import jax
import jax.numpy as jnp
from jax import lax
from jax.sharding import PartitionSpec as P

CH = 256


def from_behind(block, axis, distance):
    devices = range(lax.axis_size(axis))
    route = [(i - distance, i) for i in devices if i - distance in devices]
    return lax.ppermute(block, axis, route)


def causal(padded, kernel):
    length = padded.shape[0] - 3
    total = kernel[0] * padded[0:length].astype(jnp.float32)
    for offset in range(1, 4):
        total = total + kernel[offset] * padded[offset : offset + length].astype(jnp.float32)
    return jax.nn.silu(total).astype(jnp.bfloat16)


def body(
    tokens,
    z_weight,
    x_weight,
    bc_weight,
    step_weight,
    x_kernel,
    bc_kernel,
    step_bias,
    log_decay,
    skip_gain,
    norm_gain,
    out_weight,
):
    tok_rows = tokens.shape[0]
    heads_here = step_bias.shape[0]
    inner_width = x_weight.shape[1]
    head_size = inner_width // heads_here
    state_size = bc_weight.shape[1] // 2
    piece = lax.all_gather(tokens, "head", axis=1, tiled=True)

    def product(weight):
        return jnp.dot(piece, weight, preferred_element_type=jnp.float32)

    z_sum = product(z_weight)
    x_sum = product(x_weight)
    bc_sum = product(bc_weight)
    step_raw = product(step_weight)
    z_in = z_sum.astype(jnp.bfloat16)
    x_in = x_sum.astype(jnp.bfloat16)
    bc_in = bc_sum.astype(jnp.bfloat16)
    border = jnp.concatenate([x_in[-3:], bc_in[-3:]], axis=1)
    border = from_behind(border, "seq", 1)
    x_conv = causal(jnp.concatenate([border[:, :inner_width], x_in], axis=0), x_kernel)
    bc_conv = causal(jnp.concatenate([border[:, inner_width:], bc_in], axis=0), bc_kernel)
    blocks = tok_rows // CH
    b_map = bc_conv[:, :state_size].reshape(blocks, CH, state_size)
    c_map = bc_conv[:, state_size:].reshape(blocks, CH, state_size)
    step_size = jax.nn.softplus(step_raw + step_bias)
    rate = -jnp.exp(log_decay) * step_size
    values = x_conv.reshape(blocks, CH, heads_here, head_size)
    steps_b = step_size.reshape(blocks, CH, heads_here)
    cumulative = jnp.cumsum(rate.reshape(blocks, CH, heads_here), axis=1)
    lower = (jnp.arange(CH)[:, None] >= jnp.arange(CH)[None, :])[None, :, :, None]
    gram = jnp.einsum("ctn,csn->cts", c_map, b_map, preferred_element_type=jnp.float32)
    spread = cumulative[:, :, None, :] - cumulative[:, None, :, :]
    mixing = jnp.where(
        lower,
        gram[..., None] * jnp.exp(jnp.where(lower, spread, 0.0)) * steps_b[:, None, :, :],
        0.0,
    ).astype(jnp.bfloat16)
    intra = jnp.einsum("ctsh,cshp->cthp", mixing, values, preferred_element_type=jnp.float32)
    tails = jnp.exp(cumulative[:, -1:, :] - cumulative) * steps_b
    weighted = (values.astype(jnp.float32) * tails[..., None]).astype(jnp.bfloat16)
    local = jnp.einsum("cthp,ctn->chpn", weighted, b_map, preferred_element_type=jnp.float32)
    block_decay = jnp.exp(cumulative[:, -1, :])

    def advance(carry, item):
        state, decay = carry
        term, factor = item
        return ((factor[:, None, None] * state + term, decay * factor), (state, decay))

    zero_state = jnp.zeros((heads_here, head_size, state_size), jnp.float32)
    unit_decay = jnp.ones((heads_here,), jnp.float32)
    (shard_state, shard_decay), (local_in, decay_in) = lax.scan(
        advance, (zero_state, unit_decay), (local, block_decay)
    )

    def relay(index, carried):
        return from_behind(shard_decay[:, None, None] * carried + shard_state, "seq", 1)

    incoming = lax.fori_loop(0, lax.axis_size("seq") - 1, relay, zero_state)
    entering = local_in + decay_in[:, :, None, None] * incoming[None]
    held = entering.astype(jnp.bfloat16)
    from_state = (
        jnp.einsum("ctn,chpn->cthp", c_map, held, preferred_element_type=jnp.float32)
        * jnp.exp(cumulative)[..., None]
    )
    output_y = intra + from_state + skip_gain[None, None, :, None] * values.astype(jnp.float32)
    gated = (
        output_y.reshape(tok_rows, inner_width) * jax.nn.silu(z_in.astype(jnp.float32))
    ).astype(jnp.bfloat16)
    head_count = lax.axis_size("head")
    columns = lax.all_to_all(out_weight, "head", split_axis=1, concat_axis=0, tiled=True)
    gain_row = norm_gain.reshape(1, inner_width)
    section = lax.all_gather(gated, "head", axis=1, tiled=True)
    gain_part = lax.all_gather(gain_row, "head", axis=1, tiled=True)
    section_f = section.astype(jnp.float32)
    scaled = (section_f * gain_part.astype(jnp.float32)).astype(jnp.bfloat16)
    partial_out = jnp.dot(scaled, columns, preferred_element_type=jnp.float32)
    squares = jnp.sum(section_f * section_f, axis=1)
    meansq = squares / (inner_width * head_count)
    return (partial_out * lax.rsqrt(meansq + 1e-05)[:, None]).astype(jnp.bfloat16)


def solution(mesh):
    placed = (
        P("seq", "head"),
        P(None, "head"),
        P(None, "head"),
        P(),
        P(None, "head"),
        P(None, "head"),
        P(),
        P("head"),
        P("head"),
        P("head"),
        P("head"),
        P("head", None),
    )
    return jax.shard_map(
        body, mesh=mesh, in_specs=placed, out_specs=P("seq", "head"), check_vma=False
    )
```

profile of v0, /device:TPU:10, one launch (start us, length us, event | category | flops | bytes accessed | tf_op | source)
XLA Modules:
  0.0 403.9 jit_solution(2700277313001061849)
XLA Ops:
  6.5 0.7 all-gather.4.cloned.1.call-update
  9.4 0.8 slice_bitcast_fusion.4
  10.2 0.8 fusion.44
  11.0 148.9 %all-gather.4.cloned.1.call-done = bf16[1024,2048]{0,1:T(8,128)(2,1)} async-done(((bf16[1024,32]{0,1:T(8,128)(2,1)}), bf16[1024,2048]{0,1:T(8,128)(2,1)}) %all-gather.4.cloned.1.call-update) | async-done | bytes 4194320 | tf_op jit(solution)/shard_map/all_gather | solution.py:42
  160.0 2.8 fusion.45
  162.8 1.2 reduce-window.6
  164.3 3.6 convolution_convert_fusion
  168.0 0.9 convolution_convert_fusion.2
  169.0 1.9 collective-permute-start.1
  171.3 3.5 collective-permute-done.1
  174.8 1.0 multiply_convert_fusion
  176.2 0.3 convert_multiply_fusion.2
  176.8 8.1 %while.28 = (s32[]{:T(128)}, f32[1,64,128]{2,1,0:T(8,128)S(1)}, f32[1]{0:T(128)}, f32[4,1,64,128]{3,2,1,0:T(8,128)S(1)}, f32[4,1]{0,1:T(1,128)S(1)}, /*index=5*/...) while((s32[]{:T(128)}, f32[1,64,128]{2,1,0:T(8,128)S(1)}, f32[1]{0:T(128)}, ...), condition=%wide.region_3.4_spmd.clone, body=%wide.region_2.3_spmd.clone.sunk | while | flops 32772 | bytes 164008 | solution.py:87
  176.8 0.6 constant_dynamic-slice_fusion.2
  177.4 0.7 bitcast_add_fusion.4
  178.8 0.6 constant_dynamic-slice_fusion.2
  179.4 0.7 bitcast_add_fusion.4
  180.8 0.6 constant_dynamic-slice_fusion.2
  181.4 0.7 bitcast_add_fusion.4
  182.8 0.6 constant_dynamic-slice_fusion.2
  183.4 0.7 bitcast_add_fusion.4
  184.8 0.5 fusion.10
  185.4 36.8 %while.27 = (s32[]{:T(128)}, f32[1,64,128]{2,1,0:T(8,128)S(1)}, f32[1]{0:T(128)}, f32[1,64,128]{2,1,0:T(8,128)S(1)}, s32[]{:T(128)}) while((s32[]{:T(128)}, f32[1,64,128]{2,1,0:T(8,128)S(1)}, f32[1]{0:T(128)}, f32[1,64,128]{2,1,0:T(8,128)S(1)}, s32[]{:T(128)}) %tuple.53), condition=%wide.region_5.6_spmd, body=%wide.region_4.5_spmd.sunk | while | flops 16386 | bytes 229481 | solution.py:94
  185.4 2.1 collective-permute-start
  187.5 3.3 collective-permute-done
  190.8 1.9 collective-permute-start
  192.7 3.3 collective-permute-done
  196.0 1.9 collective-permute-start
  198.0 3.3 collective-permute-done
  201.3 1.9 collective-permute-start
  203.2 3.3 collective-permute-done
  206.5 1.9 collective-permute-start
  208.4 3.3 collective-permute-done
  211.7 1.9 collective-permute-start
  213.7 3.3 collective-permute-done
  217.0 1.9 collective-permute-start
  218.9 3.3 collective-permute-done
  222.7 3.7 multiply_convert_fusion.1
  226.5 0.3 copy.63
  226.8 1.0 reshape.305
  227.8 10.3 %all-to-all-start = ((bf16[64,2,1024]{2,1,0:T(2,128)(2,1)}), bf16[64,2,1024]{2,1,0:T(2,128)(2,1)S(1)}, u32[]{:S(2)}, u32[]{:S(2)}) async-start(bf16[64,2,1024]{2,1,0:T(2,128)(2,1)} %reshape.305), calls=%async_computation | async-start | bytes 524288 | tf_op jit(solution)/shard_map/all_to_all | solution.py:106
  238.1 1.3 dynamic-slice
  240.3 147.3 %all-reduce = bf16[4096]{0:T(1024)(128)(2,1)S(1)} all-reduce(bf16[4096]{0:T(1024)(128)(2,1)S(1)} %dynamic-update-slice), channel_id=2, replica_groups=mesh['seq'=8,'head'=64] {'head'}, use_global_device_ids=true, to_apply=%add | all-reduce | flops 4096 | bytes 16384
  387.6 0.3 reshape.306
  388.2 0.5 all_to_all.17
  388.7 5.2 %fusion.1 = f32[1024]{0:T(1024)S(1)} fusion(bf16[1024,4096]{0,1:T(8,128)(2,1)} %all-gather.6.cloned.1.call-done), kind=kLoop, calls=%fused_computation.7 | loop fusion | flops 12581888 | bytes 8392704 | tf_op jit(solution)/shard_map/reduce_sum | solution.py:113
  394.0 0.5 copy-done.2
  394.5 2.5 fusion.17
  (69 shorter events, 3.0 us)
Async XLA Ops:
  6.5 157.7 %copy-start = (bf16[2048,256]{1,0:T(8,128)(2,1)S(1)}, bf16[2048,256]{1,0:T(8,128)(2,1)}, u32[]{:S(2)}) copy-start(bf16[2048,256]{1,0:T(8,128)(2,1)} %param.19) | copy-start | bytes 3145732
  6.5 153.4 %all-gather.4.cloned.1.call-start = ((), (), s32[]{:S(2)}) async-start(), calls=%async_computation.1 | async-start | bytes 4259840 | tf_op jit(solution)/shard_map/all_gather | solution.py:42
  7.3 381.4 %all-gather.6.cloned.1.call-start = ((), (), s32[]{:S(2)}) async-start(), calls=%async_computation.2 | async-start | bytes 8519680 | tf_op jit(solution)/shard_map/all_gather | solution.py:108
  164.3 3.8 copy-start.1
  164.3 3.8 copy-start.3
  169.0 5.8 %collective-permute-start.1 = (bf16[3,320]{0,1:T(8,128)(2,1)S(1)}, bf16[3,320]{0,1:T(8,128)(2,1)S(1)}, u32[]{:S(2)}, u32[]{:S(2)}) collective-permute-start(bf16[3,320]{0,1:T(8,128)(2,1)S(1)} %pad_maximum_fusion.2), channel_id=1, source_target_pairs={{0,64},{64,128},{128,192},{192,256},{256,320},{320,384},{384,448},... | collective-permute-start | bytes 5768 | tf_op jit(solution)/shard_map/ppermute | solution.py:12
  176.2 46.5 %copy-start.4 = (bf16[2048,64]{0,1:T(8,128)(2,1)S(1)}, bf16[2048,64]{0,1:T(8,128)(2,1)}, u32[]{:S(2)}) copy-start(bf16[2048,64]{0,1:T(8,128)(2,1)} %param.17) | copy-start | bytes 786436
  185.4 41.1 %copy-start.5 = (bf16[64,2048]{1,0:T(8,128)(2,1)S(1)}, bf16[64,2048]{1,0:T(8,128)(2,1)}, u32[]{:S(2)}) copy-start(bf16[64,2048]{1,0:T(8,128)(2,1)} %param.27) | copy-start | bytes 786436
  185.4 5.4 %collective-permute-start = (f32[1,64,128]{2,1,0:T(8,128)S(1)}, f32[1,64,128]{2,1,0:T(8,128)S(1)}, u32[]{:S(2)}, u32[]{:S(2)}) collective-permute-start(f32[1,64,128]{2,1,0:T(8,128)S(1)} %multiply_add_fusion.2), channel_id=1, source_target_pairs={{0,64},{64,128},{128,192},{192,256},{256,320},{320,384},{384,448},... | collective-permute-start | bytes 98312 | tf_op jit(solution)/shard_map/while/body/eval_jaxpr/ppermute | solution.py:12
  190.8 5.2 %collective-permute-start = (f32[1,64,128]{2,1,0:T(8,128)S(1)}, f32[1,64,128]{2,1,0:T(8,128)S(1)}, u32[]{:S(2)}, u32[]{:S(2)}) collective-permute-start(f32[1,64,128]{2,1,0:T(8,128)S(1)} %multiply_add_fusion.2), channel_id=1, source_target_pairs={{0,64},{64,128},{128,192},{192,256},{256,320},{320,384},{384,448},... | collective-permute-start | bytes 98312 | tf_op jit(solution)/shard_map/while/body/eval_jaxpr/ppermute | solution.py:12
  196.0 5.2 %collective-permute-start = (f32[1,64,128]{2,1,0:T(8,128)S(1)}, f32[1,64,128]{2,1,0:T(8,128)S(1)}, u32[]{:S(2)}, u32[]{:S(2)}) collective-permute-start(f32[1,64,128]{2,1,0:T(8,128)S(1)} %multiply_add_fusion.2), channel_id=1, source_target_pairs={{0,64},{64,128},{128,192},{192,256},{256,320},{320,384},{384,448},... | collective-permute-start | bytes 98312 | tf_op jit(solution)/shard_map/while/body/eval_jaxpr/ppermute | solution.py:12
  201.3 5.2 %collective-permute-start = (f32[1,64,128]{2,1,0:T(8,128)S(1)}, f32[1,64,128]{2,1,0:T(8,128)S(1)}, u32[]{:S(2)}, u32[]{:S(2)}) collective-permute-start(f32[1,64,128]{2,1,0:T(8,128)S(1)} %multiply_add_fusion.2), channel_id=1, source_target_pairs={{0,64},{64,128},{128,192},{192,256},{256,320},{320,384},{384,448},... | collective-permute-start | bytes 98312 | tf_op jit(solution)/shard_map/while/body/eval_jaxpr/ppermute | solution.py:12
  206.5 5.2 %collective-permute-start = (f32[1,64,128]{2,1,0:T(8,128)S(1)}, f32[1,64,128]{2,1,0:T(8,128)S(1)}, u32[]{:S(2)}, u32[]{:S(2)}) collective-permute-start(f32[1,64,128]{2,1,0:T(8,128)S(1)} %multiply_add_fusion.2), channel_id=1, source_target_pairs={{0,64},{64,128},{128,192},{192,256},{256,320},{320,384},{384,448},... | collective-permute-start | bytes 98312 | tf_op jit(solution)/shard_map/while/body/eval_jaxpr/ppermute | solution.py:12
  211.7 5.2 %collective-permute-start = (f32[1,64,128]{2,1,0:T(8,128)S(1)}, f32[1,64,128]{2,1,0:T(8,128)S(1)}, u32[]{:S(2)}, u32[]{:S(2)}) collective-permute-start(f32[1,64,128]{2,1,0:T(8,128)S(1)} %multiply_add_fusion.2), channel_id=1, source_target_pairs={{0,64},{64,128},{128,192},{192,256},{256,320},{320,384},{384,448},... | collective-permute-start | bytes 98312 | tf_op jit(solution)/shard_map/while/body/eval_jaxpr/ppermute | solution.py:12
  217.0 5.2 %collective-permute-start = (f32[1,64,128]{2,1,0:T(8,128)S(1)}, f32[1,64,128]{2,1,0:T(8,128)S(1)}, u32[]{:S(2)}, u32[]{:S(2)}) collective-permute-start(f32[1,64,128]{2,1,0:T(8,128)S(1)} %multiply_add_fusion.2), channel_id=1, source_target_pairs={{0,64},{64,128},{128,192},{192,256},{256,320},{320,384},{384,448},... | collective-permute-start | bytes 98312 | tf_op jit(solution)/shard_map/while/body/eval_jaxpr/ppermute | solution.py:12
  222.4 17.6 %copy-start.6 = (bf16[64]{0:T(256)(128)(2,1)S(1)}, bf16[64]{0:T(256)(128)(2,1)}, u32[]{:S(2)}) copy-start(bf16[64]{0:T(256)(128)(2,1)} %param.26) | copy-start | bytes 388
  227.8 159.8 %all-to-all-start = ((bf16[64,2,1024]{2,1,0:T(2,128)(2,1)}), bf16[64,2,1024]{2,1,0:T(2,128)(2,1)S(1)}, u32[]{:S(2)}, u32[]{:S(2)}) async-start(bf16[64,2,1024]{2,1,0:T(2,128)(2,1)} %reshape.305), calls=%async_computation | async-start | bytes 524288 | tf_op jit(solution)/shard_map/all_to_all | solution.py:106
  388.7 5.8 %copy-start.2 = (bf16[1024,4096]{0,1:T(8,128)(2,1)S(1)}, bf16[1024,4096]{0,1:T(8,128)(2,1)}, u32[]{:S(2)}) copy-start(bf16[1024,4096]{0,1:T(8,128)(2,1)} %all-gather.6.cloned.1.call-done) | copy-start | bytes 25165828
Sparse Core Ops, SparseCore 0:
  10.3 149.6 all-gather.3
  226.6 154.3 all-gather.5
where the time goes:
time: 404 us
  waiting for transfers between devices  176 us (44%)
  blocking collectives  147 us (36%)
  starting transfers between devices  25.8 us (6%)
  between operations  16.4 us (4%)
  matrix products  14.6 us (4%)
  other arithmetic  10.6 us (3%)
  local copies, waits for them, and re-layouts  10.1 us (2%)
    all_gather x1, waiting for transfers between devices, body(): piece = lax.all_gather(tokens, 'head', axis=1, tiled=True)  149 us
    unnamed x1, blocking collectives  147 us
    ppermute x8, waiting for transfers between devices, from_behind(): return lax.ppermute(block, axis, route)  26.6 us
    ppermute x8, starting transfers between devices, from_behind(): return lax.ppermute(block, axis, route)  15.4 us
    dot_general x4, matrix products, product(): return jnp.dot(piece, weight, preferred_element_type=jnp.float32)  11.1 us
    all_to_all x1, starting transfers between devices, body(): lax.all_to_all(out_weight, 'head', split_axis=1, concat_axis=0, tiled=True)  10.3 us
  transfers between devices with their start and end apart: 11, of which 9 were waited for; matrix products, arithmetic and copies ran while one was open for 1% of the time, Pallas kernels for 0%

commit v1 on v0

--- a/solution.py
+++ b/solution.py
@@ -1,9 +1,26 @@
+import functools
 import jax
 import jax.numpy as jnp
 from jax import lax
 from jax.sharding import PartitionSpec as P
 
 CH = 256
+
+
+def create_the_tracks(original, a_name):
+    mixed_arr = jnp.concatenate(
+        jax.lax.all_to_all(
+            jnp.stack(jax.lax.axis_size(a_name) * [original], 0),
+            a_name,
+            split_axis=0,
+            concat_axis=0,
+        ),
+        1,
+    )
+    return mixed_arr
+
+
+put_area = functools.partial(create_the_tracks, a_name="head")
 
 
 def from_behind(block, axis, distance):
@@ -39,7 +56,7 @@
     inner_width = x_weight.shape[1]
     head_size = inner_width // heads_here
     state_size = bc_weight.shape[1] // 2
-    piece = lax.all_gather(tokens, "head", axis=1, tiled=True)
+    piece = put_area(tokens)
 
     def product(weight):
         return jnp.dot(piece, weight, preferred_element_type=jnp.float32)

time: 404 us -> 461 us (1.14)
  waiting for transfers between devices: 176 us -> 214 us
  starting transfers between devices: 25.8 us -> 40.4 us
    all_to_all x0 -> x1, waiting for transfers between devices: none -> 188 us  [create_the_tracks(): jax.lax.all_to_all(jnp.stack(jax.lax.axis_size(a_name) * [original], 0),...]
    all_gather x1 -> x0, waiting for transfers between devices: 149 us -> none  [body(): piece = lax.all_gather(tokens, 'head', axis=1, tiled=True)]
    all_to_all x0 -> x1, starting transfers between devices: none -> 19 us  [create_the_tracks(): jax.lax.all_to_all(jnp.stack(jax.lax.axis_size(a_name) * [original], 0),...]
where the time goes in v1:
time: 461 us
  waiting for transfers between devices  214 us (46%)
  blocking collectives  148 us (32%)
  starting transfers between devices  40.4 us (9%)
  matrix products  16.6 us (4%)
  between operations  16.4 us (4%)
  local copies, waits for them, and re-layouts  11.9 us (3%)
  other arithmetic  10.6 us (2%)
    all_to_all x1, waiting for transfers between devices, create_the_tracks(): jax.lax.all_to_all(jnp.stack(jax.lax.axis_size(a_name) * [original], 0),...  188 us
    unnamed x1, blocking collectives  148 us
    ppermute x8, waiting for transfers between devices, from_behind(): return lax.ppermute(block, axis, route)  26.6 us
    all_to_all x1, starting transfers between devices, create_the_tracks(): jax.lax.all_to_all(jnp.stack(jax.lax.axis_size(a_name) * [original], 0),...  19 us
    ppermute x8, starting transfers between devices, from_behind(): return lax.ppermute(block, axis, route)  15.4 us
    dot_general x4, matrix products, product(): return jnp.dot(piece, weight, preferred_element_type=jnp.float32)  13.1 us
  transfers between devices with their start and end apart: 11, of which 9 were waited for; matrix products, arithmetic and copies ran while one was open for 1% of the time, Pallas kernels for 0%

profile of v1, /device:TPU:10, one launch (start us, length us, event | category | flops | bytes accessed | tf_op | source)
XLA Modules:
  0.0 460.7 jit_solution(2028875510062490540)
XLA Ops:
  6.5 3.4 stack.2
  10.0 19.0 %all-to-all-start = ((bf16[64,1024,32]{1,2,0:T(8,128)(2,1)}), bf16[64,1024,32]{1,2,0:T(8,128)(2,1)}, u32[]{:S(2)}, u32[]{:S(2)}) async-start(bf16[64,1024,32]{1,2,0:T(8,128)(2,1)} %stack.2), calls=%async_computation | async-start | bytes 8388608 | tf_op jit(solution)/shard_map/all_to_all | solution.py:12
  31.1 187.8 %all-to-all-done = bf16[64,1024,32]{1,2,0:T(8,128)(2,1)} async-done(((bf16[64,1024,32]{1,2,0:T(8,128)(2,1)}), bf16[64,1024,32]{1,2,0:T(8,128)(2,1)}, u32[]{:S(2)}, u32[]{:S(2)}) %all-to-all-start) | async-done | bytes 4194336 | tf_op jit(solution)/shard_map/all_to_all | solution.py:12
  218.9 2.8 fusion.45
  221.7 1.2 reduce-window.6
  223.2 3.5 convolution_convert_fusion
  226.8 3.0 convolution_convert_fusion.2
  230.0 1.9 collective-permute-start.1
  232.2 3.5 collective-permute-done.1
  235.7 1.0 multiply_convert_fusion
  237.1 0.3 convert_multiply_fusion.2
  237.7 8.1 %while.28 = (s32[]{:T(128)}, f32[1,64,128]{2,1,0:T(8,128)S(1)}, f32[1]{0:T(128)}, f32[4,1,64,128]{3,2,1,0:T(8,128)S(1)}, f32[4,1]{0,1:T(1,128)S(1)}, /*index=5*/...) while((s32[]{:T(128)}, f32[1,64,128]{2,1,0:T(8,128)S(1)}, f32[1]{0:T(128)}, ...), condition=%wide.region_3.4_spmd.clone, body=%wide.region_2.3_spmd.clone.sunk | while | flops 32772 | bytes 164008 | solution.py:104
  237.8 0.6 constant_dynamic-slice_fusion.2
  238.4 0.7 bitcast_add_fusion.4
  239.8 0.6 constant_dynamic-slice_fusion.2
  240.3 0.7 bitcast_add_fusion.4
  241.8 0.6 constant_dynamic-slice_fusion.2
  242.4 0.7 bitcast_add_fusion.4
  243.8 0.6 constant_dynamic-slice_fusion.2
  244.4 0.7 bitcast_add_fusion.4
  245.8 0.5 fusion.10
  246.4 36.8 %while.27 = (s32[]{:T(128)}, f32[1,64,128]{2,1,0:T(8,128)S(1)}, f32[1]{0:T(128)}, f32[1,64,128]{2,1,0:T(8,128)S(1)}, s32[]{:T(128)}) while((s32[]{:T(128)}, f32[1,64,128]{2,1,0:T(8,128)S(1)}, f32[1]{0:T(128)}, f32[1,64,128]{2,1,0:T(8,128)S(1)}, s32[]{:T(128)}) %tuple.53), condition=%wide.region_5.6_spmd, body=%wide.region_4.5_spmd.sunk | while | flops 16386 | bytes 229481 | solution.py:111
  246.4 2.1 collective-permute-start
  248.4 3.3 collective-permute-done
  251.8 1.9 collective-permute-start
  253.7 3.3 collective-permute-done
  257.0 1.9 collective-permute-start
  258.9 3.3 collective-permute-done
  262.2 1.9 collective-permute-start
  264.1 3.3 collective-permute-done
  267.4 1.9 collective-permute-start
  269.4 3.3 collective-permute-done
  272.7 1.9 collective-permute-start
  274.6 3.3 collective-permute-done
  277.9 1.9 collective-permute-start
  279.8 3.3 collective-permute-done
  283.1 0.3 fusion.12
  283.6 3.7 multiply_convert_fusion.1
  287.4 0.3 copy.64
  287.7 1.0 reshape.315
  288.7 6.0 %all-to-all-start.1 = ((bf16[64,2,1024]{2,1,0:T(2,128)(2,1)}), bf16[64,2,1024]{2,1,0:T(2,128)(2,1)S(1)}, u32[]{:S(2)}, u32[]{:S(2)}) async-start(bf16[64,2,1024]{2,1,0:T(2,128)(2,1)} %reshape.315), calls=%async_computation.1 | async-start | bytes 524288 | tf_op jit(solution)/shard_map/all_to_all | solution.py:123
  294.7 1.3 dynamic-slice
  296.9 147.5 %all-reduce = bf16[4096]{0:T(1024)(128)(2,1)S(1)} all-reduce(bf16[4096]{0:T(1024)(128)(2,1)S(1)} %dynamic-update-slice), channel_id=2, replica_groups=mesh['seq'=8,'head'=64] {'head'}, use_global_device_ids=true, to_apply=%add | all-reduce | flops 4096 | bytes 16384
  444.4 0.3 reshape.316
  445.0 0.5 all_to_all.21
  445.5 5.2 %fusion.1 = f32[1024]{0:T(1024)S(1)} fusion(bf16[1024,4096]{0,1:T(8,128)(2,1)} %all-gather.3.cloned.1.call-done), kind=kLoop, calls=%fused_computation.7 | loop fusion | flops 12581888 | bytes 8392704 | tf_op jit(solution)/shard_map/reduce_sum | solution.py:130
  450.8 0.5 copy-done.1
  451.3 2.5 fusion.17
  (73 shorter events, 2.8 us)
Async XLA Ops:
  6.5 216.6 %copy-start = (bf16[2048,256]{1,0:T(8,128)(2,1)S(1)}, bf16[2048,256]{1,0:T(8,128)(2,1)}, u32[]{:S(2)}) copy-start(bf16[2048,256]{1,0:T(8,128)(2,1)} %param.19) | copy-start | bytes 3145732
  10.0 21.1 %copy-start.7 = (f32[4,64]{1,0:T(4,128)S(1)}, f32[4,64]{1,0:T(4,128)}, u32[]{:S(2)}) copy-start(f32[4,64]{1,0:T(4,128)} %param.21) | copy-start | bytes 3076
  10.0 21.1 %copy-start.6 = (f32[4,256]{1,0:T(4,128)S(1)}, f32[4,256]{1,0:T(4,128)}, u32[]{:S(2)}) copy-start(f32[4,256]{1,0:T(4,128)} %param.22) | copy-start | bytes 12292
  10.0 208.9 %copy-start.5 = (bf16[2048,1]{0,1:T(2,128)(2,1)S(1)}, bf16[2048,1]{0,1:T(2,128)(2,1)}, u32[]{:S(2)}) copy-start(bf16[2048,1]{0,1:T(2,128)(2,1)} %param.20) | copy-start | bytes 12292
  10.0 208.9 %all-to-all-start = ((bf16[64,1024,32]{1,2,0:T(8,128)(2,1)}), bf16[64,1024,32]{1,2,0:T(8,128)(2,1)}, u32[]{:S(2)}, u32[]{:S(2)}) async-start(bf16[64,1024,32]{1,2,0:T(8,128)(2,1)} %stack.2), calls=%async_computation | async-start | bytes 8388608 | tf_op jit(solution)/shard_map/all_to_all | solution.py:12
  28.9 416.6 %all-gather.3.cloned.1.call-start = ((), (), s32[]{:S(2)}) async-start(), calls=%async_computation.2 | async-start | bytes 8519680 | tf_op jit(solution)/shard_map/all_gather | solution.py:125
  223.2 3.6 copy-start.2
  230.0 5.8 %collective-permute-start.1 = (bf16[3,320]{0,1:T(8,128)(2,1)S(1)}, bf16[3,320]{0,1:T(8,128)(2,1)S(1)}, u32[]{:S(2)}, u32[]{:S(2)}) collective-permute-start(bf16[3,320]{0,1:T(8,128)(2,1)S(1)} %pad_maximum_fusion.2), channel_id=1, source_target_pairs={{0,64},{64,128},{128,192},{192,256},{256,320},{320,384},{384,448},... | collective-permute-start | bytes 5768 | tf_op jit(solution)/shard_map/ppermute | solution.py:29
  237.1 46.5 %copy-start.3 = (bf16[2048,64]{0,1:T(8,128)(2,1)S(1)}, bf16[2048,64]{0,1:T(8,128)(2,1)}, u32[]{:S(2)}) copy-start(bf16[2048,64]{0,1:T(8,128)(2,1)} %param.17) | copy-start | bytes 786436
  246.3 41.1 %copy-start.4 = (bf16[64,2048]{1,0:T(8,128)(2,1)S(1)}, bf16[64,2048]{1,0:T(8,128)(2,1)}, u32[]{:S(2)}) copy-start(bf16[64,2048]{1,0:T(8,128)(2,1)} %param.27) | copy-start | bytes 786436
  246.4 5.4 %collective-permute-start = (f32[1,64,128]{2,1,0:T(8,128)S(1)}, f32[1,64,128]{2,1,0:T(8,128)S(1)}, u32[]{:S(2)}, u32[]{:S(2)}) collective-permute-start(f32[1,64,128]{2,1,0:T(8,128)S(1)} %multiply_add_fusion.2), channel_id=1, source_target_pairs={{0,64},{64,128},{128,192},{192,256},{256,320},{320,384},{384,448},... | collective-permute-start | bytes 98312 | tf_op jit(solution)/shard_map/while/body/eval_jaxpr/ppermute | solution.py:29
  251.8 5.2 %collective-permute-start = (f32[1,64,128]{2,1,0:T(8,128)S(1)}, f32[1,64,128]{2,1,0:T(8,128)S(1)}, u32[]{:S(2)}, u32[]{:S(2)}) collective-permute-start(f32[1,64,128]{2,1,0:T(8,128)S(1)} %multiply_add_fusion.2), channel_id=1, source_target_pairs={{0,64},{64,128},{128,192},{192,256},{256,320},{320,384},{384,448},... | collective-permute-start | bytes 98312 | tf_op jit(solution)/shard_map/while/body/eval_jaxpr/ppermute | solution.py:29
  257.0 5.2 %collective-permute-start = (f32[1,64,128]{2,1,0:T(8,128)S(1)}, f32[1,64,128]{2,1,0:T(8,128)S(1)}, u32[]{:S(2)}, u32[]{:S(2)}) collective-permute-start(f32[1,64,128]{2,1,0:T(8,128)S(1)} %multiply_add_fusion.2), channel_id=1, source_target_pairs={{0,64},{64,128},{128,192},{192,256},{256,320},{320,384},{384,448},... | collective-permute-start | bytes 98312 | tf_op jit(solution)/shard_map/while/body/eval_jaxpr/ppermute | solution.py:29
  262.2 5.2 %collective-permute-start = (f32[1,64,128]{2,1,0:T(8,128)S(1)}, f32[1,64,128]{2,1,0:T(8,128)S(1)}, u32[]{:S(2)}, u32[]{:S(2)}) collective-permute-start(f32[1,64,128]{2,1,0:T(8,128)S(1)} %multiply_add_fusion.2), channel_id=1, source_target_pairs={{0,64},{64,128},{128,192},{192,256},{256,320},{320,384},{384,448},... | collective-permute-start | bytes 98312 | tf_op jit(solution)/shard_map/while/body/eval_jaxpr/ppermute | solution.py:29
  267.4 5.2 %collective-permute-start = (f32[1,64,128]{2,1,0:T(8,128)S(1)}, f32[1,64,128]{2,1,0:T(8,128)S(1)}, u32[]{:S(2)}, u32[]{:S(2)}) collective-permute-start(f32[1,64,128]{2,1,0:T(8,128)S(1)} %multiply_add_fusion.2), channel_id=1, source_target_pairs={{0,64},{64,128},{128,192},{192,256},{256,320},{320,384},{384,448},... | collective-permute-start | bytes 98312 | tf_op jit(solution)/shard_map/while/body/eval_jaxpr/ppermute | solution.py:29
  272.7 5.2 %collective-permute-start = (f32[1,64,128]{2,1,0:T(8,128)S(1)}, f32[1,64,128]{2,1,0:T(8,128)S(1)}, u32[]{:S(2)}, u32[]{:S(2)}) collective-permute-start(f32[1,64,128]{2,1,0:T(8,128)S(1)} %multiply_add_fusion.2), channel_id=1, source_target_pairs={{0,64},{64,128},{128,192},{192,256},{256,320},{320,384},{384,448},... | collective-permute-start | bytes 98312 | tf_op jit(solution)/shard_map/while/body/eval_jaxpr/ppermute | solution.py:29
  277.9 5.2 %collective-permute-start = (f32[1,64,128]{2,1,0:T(8,128)S(1)}, f32[1,64,128]{2,1,0:T(8,128)S(1)}, u32[]{:S(2)}, u32[]{:S(2)}) collective-permute-start(f32[1,64,128]{2,1,0:T(8,128)S(1)} %multiply_add_fusion.2), channel_id=1, source_target_pairs={{0,64},{64,128},{128,192},{192,256},{256,320},{320,384},{384,448},... | collective-permute-start | bytes 98312 | tf_op jit(solution)/shard_map/while/body/eval_jaxpr/ppermute | solution.py:29
  283.4 13.2 %copy-start.8 = (bf16[64]{0:T(256)(128)(2,1)S(1)}, bf16[64]{0:T(256)(128)(2,1)}, u32[]{:S(2)}) copy-start(bf16[64]{0:T(256)(128)(2,1)} %param.26) | copy-start | bytes 388
  288.7 155.7 %all-to-all-start.1 = ((bf16[64,2,1024]{2,1,0:T(2,128)(2,1)}), bf16[64,2,1024]{2,1,0:T(2,128)(2,1)S(1)}, u32[]{:S(2)}, u32[]{:S(2)}) async-start(bf16[64,2,1024]{2,1,0:T(2,128)(2,1)} %reshape.315), calls=%async_computation.1 | async-start | bytes 524288 | tf_op jit(solution)/shard_map/all_to_all | solution.py:123
  445.5 5.8 %copy-start.1 = (bf16[1024,4096]{0,1:T(8,128)(2,1)S(1)}, bf16[1024,4096]{0,1:T(8,128)(2,1)}, u32[]{:S(2)}) copy-start(bf16[1024,4096]{0,1:T(8,128)(2,1)} %all-gather.3.cloned.1.call-done) | copy-start | bytes 25165828
Sparse Core Ops, SparseCore 0:
  287.5 149.4 all-gather.2
